TPU v7x, 32 devices: a whole 2x2x4 slice. The times are simulated.
32 devices in a mesh: scene: 2 (over y), ctx: 4 (over x, core), head: 4 (over z).
Axes of the slice: x: 2, y: 2, z: 4, core: 2. Of those that a mesh axis runs over, the one named last changes fastest.
Arguments:
- frames_in: float32 [8192, 1024], P(('scene', 'ctx')), parts along dimension 0, may hold values from -6 to 6
- merge_index: int32 [8192], P(('scene', 'ctx')), parts along dimension 0, may hold values from 0 to 1023, as said below
- frame_query: float32 [1024, 1024], P(None, 'head'), may hold values from -1 to 1
- frame_key: float32 [1024, 1024], P(None, 'head'), may hold values from -1 to 1
- frame_value: float32 [1024, 1024], P(None, 'head'), may hold values from -0.1875 to 0.1875
- frame_out: float32 [1024, 1024], P('head'), may hold values from -0.1875 to 0.1875
- global_query: float32 [1024, 1024], P(None, 'head'), may hold values from -1 to 1
- global_key: float32 [1024, 1024], P(None, 'head'), may hold values from -1 to 1
- global_value: float32 [1024, 1024], P(None, 'head'), may hold values from -0.1875 to 0.1875
- global_out: float32 [1024, 1024], P('head'), may hold values from -0.1875 to 0.1875
Outputs:
- refined: float32 [8192, 1024], P(('scene', 'ctx'), 'head'), parts along dimension 0
- merged_tokens: float32 [2048, 1024], P(('scene', 'ctx'), 'head'), parts along dimension 0
There are 2 independent parts, one for each index of `scene`. A program takes and returns all parts, laid end to end along the dimension named above; an argument that names none is the same for every part. Nothing has to cross between parts.
Inputs may be any that keep to these rules, and one draw needn't show every extreme that they name: `merge_index`: each of the 1024 merged tokens is named by at least one patch; merged tokens i * 256 to (i + 1) * 256 - 1 belong to index i of ctx; of the 1024 patches of one index of ctx at most 512 name merged tokens of any one index of ctx, exactly 512 for some index; the merged tokens of each index of ctx are named by exactly 1024 patches in all.
All inputs are finite; a program needn't handle non-finite values.
Results may differ from a plain program's by a relative error of at most 0.0003.
Values sent between devices are 32-bit elements; how exact they have to be, the bound alone decides.
A program may use at most 64 MiB of HBM per device.

v0:
```python
import functools

import jax
import jax.numpy as jnp
from jax import lax
from jax.experimental import pallas as pl
from jax.experimental.pallas import tpu as pltpu
from jax.sharding import PartitionSpec as P

HEAD_DIM = 64
PATCHES = 256
MESH = pl.DeviceIdType.MESH


def split(x):
    high = x.astype(jnp.bfloat16)
    return high, (x - high.astype(jnp.float32)).astype(jnp.bfloat16)


def dot(a, b, contract=((1,), (0,))):
    return lax.dot_general(a, b, (contract, ((), ())), preferred_element_type=jnp.float32)


def dot3(a, b, contract=((1,), (0,))):
    (a_high, a_low), (b_high, b_low) = a, b
    return (
        dot(a_high, b_high, contract) + dot(a_high, b_low, contract) + dot(a_low, b_high, contract)
    )


def layer_norm(entries):
    center = entries - jnp.mean(entries, axis=-1, keepdims=True)
    spread = jnp.mean(center * center, axis=-1, keepdims=True)
    return center * lax.rsqrt(spread + 1e-06)


def attend(query, key, value):
    scores = dot3(split(query * HEAD_DIM ** (-0.5)), split(key), ((1,), (1,)))
    weights = jnp.exp(scores - jnp.max(scores, axis=-1, keepdims=True))
    total = jnp.sum(weights, axis=-1, keepdims=True)
    return dot3(split(weights), split(value)) / total


def kernel(
    n, m,
    frames, index_row, index_col, fq, fk, fv, fo, gq, gk, gv, go,
    refined, merged_tokens,
    fw_high, fw_low, gw_high, gw_low, out_high, out_low,
    out_all, attended, frame_parts, frame_recv, att_parts, att_recv,
    frames_sum, att_sum, frames_full, att_full, merged,
    row_part, row_out, states, kv_all, g_att, upd_part, upd_recv, upd_all,
    out_sems, out_a, out_b, fs_sems, fz_sems, as_sems, az_sems, ra_sems, rb_sems,
    kv_a, kv_b, up_sems, ug_a, ug_b,
):
    me = lax.axis_index("head")
    ctx = lax.axis_index("ctx")
    tokens, width = frames.shape
    local = fq.shape[1]
    heads = local // HEAD_DIM
    rows = tokens // 4
    head_rows = tokens // n
    share = local // m
    frame_count = tokens // PATCHES
    mate = ctx + 1 - 2 * lax.rem(ctx, 2)
    pending = []

    def to(axis, target, src, dst, sems, i):
        copy = pltpu.make_async_remote_copy(
            src_ref=src, dst_ref=dst, send_sem=sems.at[0, i], recv_sem=sems.at[1, i],
            device_id={axis: target}, device_id_type=MESH,
        )
        copy.start()
        pending.append(copy)
        return copy

    def columns(i):
        return pl.ds(pl.multiple_of(i * local, local), local)

    def block_rows(i, size):
        return pl.ds(pl.multiple_of(i * size, size), size)

    def peer(base, shift, size):
        return lax.rem(base + shift, size)

    def arrive(copies):
        for copy in copies:
            copy.wait_recv()

    def gather_first(buf, sems):
        return [
            to("ctx", peer(ctx, s, m), buf.at[ctx], buf.at[ctx], sems, s // 2)
            for s in range(2, m, 2)
        ]

    def gather_second(buf, sems):
        return [
            to("ctx", mate, buf.at[peer(ctx, s, m)], buf.at[peer(ctx, s, m)], sems, s // 2)
            for s in range(0, m, 2)
        ]

    barrier = pltpu.get_barrier_semaphore()
    for s in range(1, n):
        pl.semaphore_signal(
            barrier, inc=1, device_id={"head": peer(me, s, n)}, device_id_type=MESH
        )
    for s in range(1, m):
        pl.semaphore_signal(
            barrier, inc=1, device_id={"ctx": peer(ctx, s, m)}, device_id_type=MESH
        )
    pl.semaphore_wait(barrier, n - 1 + m - 1)

    own_share = fo.at[block_rows(ctx, share), :]
    out_copies = [
        to("head", peer(me, s, n), own_share, out_all.at[ctx, me], out_sems, s)
        for s in range(1, n)
    ]
    out_all[ctx, me] = fo[block_rows(ctx, share), :]

    def one_hot(owner):
        ids = owner * rows + lax.broadcasted_iota(jnp.int32, (rows, tokens), 0)
        return ids == index_row[...]

    source = split(frames[:, columns(me)])
    frame_copies = []
    for s in [*range(1, m), 0]:
        hot = one_hot(peer(ctx, s, m)).astype(jnp.float32)
        table = hot.astype(jnp.bfloat16)
        frame_parts[s, :, :local] = dot(table, source[0]) + dot(table, source[1])
        frame_parts[s, :, local:] = jnp.broadcast_to(
            jnp.sum(hot, axis=1, keepdims=True), (rows, 128)
        )
        if s:
            frame_copies.append(
                to("ctx", peer(ctx, s, m), frame_parts.at[s], frame_recv.at[s], fs_sems, s)
            )

    for i, ref in enumerate((fq, fk, fv)):
        high, low = split(ref[...])
        fw_high[:, i * local : (i + 1) * local] = high
        fw_low[:, i * local : (i + 1) * local] = low

    def one_frame(f, carry):
        here = pl.ds(pl.multiple_of(f * PATCHES, PATCHES), PATCHES)
        normed = split(layer_norm(frames[here, :]))
        qkv = dot3(normed, (fw_high[...], fw_low[...]))
        for h in range(heads):
            at = h * HEAD_DIM
            attended[here, at : at + HEAD_DIM] = attend(
                qkv[:, at : at + HEAD_DIM],
                qkv[:, local + at : local + at + HEAD_DIM],
                qkv[:, 2 * local + at : 2 * local + at + HEAD_DIM],
            )
        return carry

    half = frame_count // 2
    lax.fori_loop(0, half, one_frame, 0)
    arrive(frame_copies)
    total = frame_parts[0]
    for s in range(1, m):
        total += frame_recv[s]
    counts = total[:, local : local + 1]
    frames_sum[...] = total[:, :local] / counts
    frames_full[:, columns(me)] = frames_sum[...]
    sum_copies = [
        to("head", peer(me, s, n), frames_sum, frames_full.at[:, columns(me)], fz_sems, s)
        for s in range(1, n)
    ]
    lax.fori_loop(half, frame_count, one_frame, 0)

    source = split(attended[...])
    att_copies = []
    for s in [*range(1, m), 0]:
        table = one_hot(peer(ctx, s, m)).astype(jnp.float32).astype(jnp.bfloat16)
        att_parts[s] = dot(table, source[0]) + dot(table, source[1])
        if s:
            att_copies.append(
                to("ctx", peer(ctx, s, m), att_parts.at[s], att_recv.at[s], as_sems, s)
            )
    for i, ref in enumerate((gq, gk, gv)):
        high, low = split(ref[...])
        gw_high[:, i * local : (i + 1) * local] = high
        gw_low[:, i * local : (i + 1) * local] = low
    arrive(out_copies)
    out_copies = gather_first(out_all, out_a)
    arrive(att_copies)
    total = att_parts[0]
    for s in range(1, m):
        total += att_recv[s]
    att_sum[...] = total / counts
    att_full[:, columns(me)] = att_sum[...]
    att_copies = [
        to("head", peer(me, s, n), att_sum, att_full.at[:, columns(me)], az_sems, s)
        for s in range(1, n)
    ]

    row_copies = [
        to(
            "head", peer(me, s, n), attended.at[block_rows(peer(me, s, n), head_rows), :],
            row_part.at[:, columns(me)], ra_sems, s,
        )
        for s in range(1, n)
    ]
    row_part[:, columns(me)] = attended[block_rows(me, head_rows), :]

    arrive(out_copies)
    out_copies = gather_second(out_all, out_b)
    arrive(out_copies)
    for i in range(n):
        high, low = split(out_all[:, i].reshape(local, width))
        out_high[i * local : (i + 1) * local, :] = high
        out_low[i * local : (i + 1) * local, :] = low
    projection = (out_high, out_low)

    arrive(sum_copies)
    arrive(att_copies)
    full = frames_full[...] + dot3(
        split(att_full[...]), (projection[0][...], projection[1][...])
    )
    att_full[...] = full
    merged[...] = att_full[:, columns(me)]
    normed = split(layer_norm(full))
    kv_all[ctx] = dot3(normed, (gw_high[:, local:], gw_low[:, local:]))
    kv_copies = gather_first(kv_all, kv_a)
    query = dot3(normed, (gw_high[:, :local], gw_low[:, :local]))
    go_pair = split(go[...])
    arrive(kv_copies)
    kv_copies = gather_second(kv_all, kv_b)

    arrive(row_copies)
    row_out[...] = dot3(split(row_part[...]), (projection[0][...], projection[1][...]))
    back_copies = [
        to(
            "head", peer(me, s, n), row_out.at[:, columns(peer(me, s, n))],
            states.at[block_rows(me, head_rows), :], rb_sems, s,
        )
        for s in range(1, n)
    ]
    states[block_rows(me, head_rows), :] = row_out[:, columns(me)]

    arrive(kv_copies)
    for h in range(heads):
        at = h * HEAD_DIM
        g_att[:, at : at + HEAD_DIM] = attend(
            query[:, at : at + HEAD_DIM],
            kv_all[:, :, at : at + HEAD_DIM].reshape(m * rows, HEAD_DIM),
            kv_all[:, :, local + at : local + at + HEAD_DIM].reshape(m * rows, HEAD_DIM),
        )
    upd_part[...] = dot3(split(g_att[...]), go_pair)
    upd_copies = [
        to(
            "head", peer(me, s, n), upd_part.at[:, columns(peer(me, s, n))],
            upd_recv.at[s], up_sems, s,
        )
        for s in range(1, n)
    ]
    update = upd_part[:, columns(me)]
    arrive(upd_copies)
    for s in range(1, n):
        update += upd_recv[s]
    upd_all[ctx] = update
    upd_copies = gather_first(upd_all, ug_a)
    merged_tokens[...] = merged[...] + update
    arrive(upd_copies)
    upd_copies = gather_second(upd_all, ug_b)
    arrive(back_copies)
    arrive(upd_copies)
    source = split(upd_all[...].reshape(m * rows, local))

    def spread(f, carry):
        here = pl.ds(pl.multiple_of(f * PATCHES, PATCHES), PATCHES)
        ids = lax.broadcasted_iota(jnp.int32, (PATCHES, m * rows), 1)
        table = (ids == index_col[here, :]).astype(jnp.float32).astype(jnp.bfloat16)
        refined[here, :] = (
            frames[here, columns(me)]
            + states[here, :]
            + (dot(table, source[0]) + dot(table, source[1]))
        )
        return carry

    lax.fori_loop(0, frame_count, spread, 0)
    for copy in pending:
        copy.wait_send()


def per_device(frames_in, merge_index, *weights):
    n = lax.axis_size("head")
    m = lax.axis_size("ctx")
    tokens, width = frames_in.shape
    local = weights[0].shape[1]
    rows = tokens // 4
    head_rows = tokens // n
    share = local // m
    f32, bf16 = jnp.float32, jnp.bfloat16

    def sems(count):
        return pltpu.SemaphoreType.DMA((2, count))

    scratch = [
        pltpu.VMEM((width, 3 * local), bf16),
        pltpu.VMEM((width, 3 * local), bf16),
        pltpu.VMEM((width, 3 * local), bf16),
        pltpu.VMEM((width, 3 * local), bf16),
        pltpu.VMEM((n * local, width), bf16),
        pltpu.VMEM((n * local, width), bf16),
        pltpu.VMEM((m, n, share, width), f32),
        pltpu.VMEM((tokens, local), f32),
        pltpu.VMEM((m, rows, local + 128), f32),
        pltpu.VMEM((m, rows, local + 128), f32),
        pltpu.VMEM((m, rows, local), f32),
        pltpu.VMEM((m, rows, local), f32),
        pltpu.VMEM((rows, local), f32),
        pltpu.VMEM((rows, local), f32),
        pltpu.VMEM((rows, width), f32),
        pltpu.VMEM((rows, width), f32),
        pltpu.VMEM((rows, local), f32),
        pltpu.VMEM((head_rows, width), f32),
        pltpu.VMEM((head_rows, width), f32),
        pltpu.VMEM((tokens, local), f32),
        pltpu.VMEM((m, rows, 2 * local), f32),
        pltpu.VMEM((rows, local), f32),
        pltpu.VMEM((rows, width), f32),
        pltpu.VMEM((n, rows, local), f32),
        pltpu.VMEM((m, rows, local), f32),
        sems(n), sems(m), sems(m), sems(m), sems(n), sems(m), sems(n), sems(n), sems(n),
        sems(m), sems(m), sems(n), sems(m), sems(m),
    ]
    vmem = pl.BlockSpec(memory_space=pltpu.VMEM)
    return pl.pallas_call(
        functools.partial(kernel, n, m),
        out_shape=(
            jax.ShapeDtypeStruct((tokens, local), f32),
            jax.ShapeDtypeStruct((rows, local), f32),
        ),
        in_specs=[vmem] * (3 + len(weights)),
        out_specs=(vmem, vmem),
        scratch_shapes=scratch,
        compiler_params=pltpu.CompilerParams(
            collective_id=0, has_side_effects=True, vmem_limit_bytes=60 * 1024 * 1024
        ),
    )(frames_in, merge_index.reshape(1, tokens), merge_index.reshape(tokens, 1), *weights)


def solution(mesh):
    placed = (
        P(("scene", "ctx"), None),
        P(("scene", "ctx")),
        P(None, "head"),
        P(None, "head"),
        P(None, "head"),
        P("head", None),
        P(None, "head"),
        P(None, "head"),
        P(None, "head"),
        P("head", None),
    )
    return jax.shard_map(
        per_device,
        mesh=mesh,
        in_specs=placed,
        out_specs=(P(("scene", "ctx"), "head"), P(("scene", "ctx"), "head")),
        check_vma=False,
    )
```

profile of v0, /device:TPU:29, one launch (start us, length us, event | category | flops | bytes accessed | tf_op | source)
XLA Modules:
  0.0 169.4 jit_solution(12382116304027786433)
XLA Ops:
  0.6 1.7 %copy.12.index_col = s32[1024,1]{1,0:T(8,128)} copy(s32[1024,1]{0,1:T(1,128)} %bitcast.2) | data formatting | bytes 8192 | tf_op jit(solution)/shard_map/reshape | solution.py:340
  2.3 163.1 %shard_map.113 = (f32[1024,256]{1,0:T(8,128)}, f32[256,256]{1,0:T(8,128)}) custom-call(f32[1024,1024]{1,0:T(8,128)} %frames.1, s32[1,1024]{1,0:T(1,128)} %bitcast.3, s32[1024,1]{1,0:T(8,128)} %copy.12.index_col, f32[1024,256]{1,0:T(8,128)} %fq.1, f32[1024,256]{1,0:T(8,128)} %fk.1, f32[1024,256]{1,0:T(8,128)} %fv.1, f32[256,1024]{1,0:T(8,128)} %fo.1, ...), custom_call_target="tpu_custom_call" | custom-call | tf_op jit(solution)/shard_map/pallas_call | solution.py:328
  165.5 2.3 %copy.15 = f32[1024,256]{1,0:T(8,128)} copy(f32[1024,256]{1,0:T(8,128)} %get-tuple-element.4) | data formatting | bytes 2097152
  167.7 1.7 copy.16
where the time goes:
time: 170 us; the launch traced here: 169 us
  Pallas kernels  163 us (96%)
  local copies, waits for them, and re-layouts  5.64 us (3%)
    pallas_call x1, Pallas kernels, per_device(): pl.pallas_call(functools.partial(kernel, n, m), out_shape=(jax.ShapeDtype...  163 us
    unnamed x2, local copies, waits for them, and re-layouts  3.93 us

commit v1 on v0

--- a/solution.py
+++ b/solution.py
@@ -86,17 +86,20 @@
         for copy in copies:
             copy.wait_recv()
 
-    def gather_first(buf, sems):
-        return [
+    def gather_first(buf, sems, mate_sems):
+        far = [
             to("ctx", peer(ctx, s, m), buf.at[ctx], buf.at[ctx], sems, s // 2)
             for s in range(2, m, 2)
         ]
-
-    def gather_second(buf, sems):
-        return [
-            to("ctx", mate, buf.at[peer(ctx, s, m)], buf.at[peer(ctx, s, m)], sems, s // 2)
-            for s in range(0, m, 2)
-        ]
+        return far, [to("ctx", mate, buf.at[ctx], buf.at[ctx], mate_sems, 0)]
+
+    def gather_second(buf, copies, mate_sems):
+        far, near = copies
+        for i, s in enumerate(range(2, m, 2)):
+            far[i].wait_recv()
+            source = buf.at[peer(ctx, m - s, m)]
+            near.append(to("ctx", mate, source, source, mate_sems, i + 1))
+        return near
 
     barrier = pltpu.get_barrier_semaphore()
     for s in range(1, n):
@@ -167,6 +170,15 @@
     ]
     lax.fori_loop(half, frame_count, one_frame, 0)
 
+    row_copies = [
+        to(
+            "head", peer(me, s, n), attended.at[block_rows(peer(me, s, n), head_rows), :],
+            row_part.at[:, columns(me)], ra_sems, s,
+        )
+        for s in range(1, n)
+    ]
+    row_part[:, columns(me)] = attended[block_rows(me, head_rows), :]
+
     source = split(attended[...])
     att_copies = []
     for s in [*range(1, m), 0]:
@@ -181,7 +193,7 @@
         gw_high[:, i * local : (i + 1) * local] = high
         gw_low[:, i * local : (i + 1) * local] = low
     arrive(out_copies)
-    out_copies = gather_first(out_all, out_a)
+    out_copies = gather_first(out_all, out_a, out_b)
     arrive(att_copies)
     total = att_parts[0]
     for s in range(1, m):
@@ -193,17 +205,7 @@
         for s in range(1, n)
     ]
 
-    row_copies = [
-        to(
-            "head", peer(me, s, n), attended.at[block_rows(peer(me, s, n), head_rows), :],
-            row_part.at[:, columns(me)], ra_sems, s,
-        )
-        for s in range(1, n)
-    ]
-    row_part[:, columns(me)] = attended[block_rows(me, head_rows), :]
-
-    arrive(out_copies)
-    out_copies = gather_second(out_all, out_b)
+    out_copies = gather_second(out_all, out_copies, out_b)
     arrive(out_copies)
     for i in range(n):
         high, low = split(out_all[:, i].reshape(local, width))
@@ -220,12 +222,7 @@
     merged[...] = att_full[:, columns(me)]
     normed = split(layer_norm(full))
     kv_all[ctx] = dot3(normed, (gw_high[:, local:], gw_low[:, local:]))
-    kv_copies = gather_first(kv_all, kv_a)
-    query = dot3(normed, (gw_high[:, :local], gw_low[:, :local]))
-    go_pair = split(go[...])
-    arrive(kv_copies)
-    kv_copies = gather_second(kv_all, kv_b)
-
+    kv_copies = gather_first(kv_all, kv_a, kv_b)
     arrive(row_copies)
     row_out[...] = dot3(split(row_part[...]), (projection[0][...], projection[1][...]))
     back_copies = [
@@ -236,34 +233,55 @@
         for s in range(1, n)
     ]
     states[block_rows(me, head_rows), :] = row_out[:, columns(me)]
+    query = dot3(normed, (gw_high[:, :local], gw_low[:, :local]))
+    go_pair = split(go[...])
+    kv_copies = gather_second(kv_all, kv_copies, kv_b)
 
     arrive(kv_copies)
-    for h in range(heads):
-        at = h * HEAD_DIM
-        g_att[:, at : at + HEAD_DIM] = attend(
-            query[:, at : at + HEAD_DIM],
-            kv_all[:, :, at : at + HEAD_DIM].reshape(m * rows, HEAD_DIM),
-            kv_all[:, :, local + at : local + at + HEAD_DIM].reshape(m * rows, HEAD_DIM),
-        )
-    upd_part[...] = dot3(split(g_att[...]), go_pair)
-    upd_copies = [
-        to(
-            "head", peer(me, s, n), upd_part.at[:, columns(peer(me, s, n))],
-            upd_recv.at[s], up_sems, s,
-        )
-        for s in range(1, n)
-    ]
-    update = upd_part[:, columns(me)]
-    arrive(upd_copies)
-    for s in range(1, n):
-        update += upd_recv[s]
-    upd_all[ctx] = update
-    upd_copies = gather_first(upd_all, ug_a)
-    merged_tokens[...] = merged[...] + update
-    arrive(upd_copies)
-    upd_copies = gather_second(upd_all, ug_b)
+    part = rows // 2
+    halves = []
+    for half in range(2):
+        here = slice(half * part, (half + 1) * part)
+        for h in range(heads):
+            at = h * HEAD_DIM
+            g_att[here, at : at + HEAD_DIM] = attend(
+                query[here, at : at + HEAD_DIM],
+                kv_all[:, :, at : at + HEAD_DIM].reshape(m * rows, HEAD_DIM),
+                kv_all[:, :, local + at : local + at + HEAD_DIM].reshape(m * rows, HEAD_DIM),
+            )
+        upd_part[here, :] = dot3(split(g_att[here, :]), go_pair)
+        halves.append([
+            to(
+                "head", peer(me, s, n),
+                upd_part.at[pl.ds(half * part, part), columns(peer(me, s, n))],
+                upd_recv.at[s, pl.ds(half * part, part)], up_sems, half * n + s,
+            )
+            for s in range(1, n)
+        ])
+    firsts = []
+    for half in range(2):
+        here = pl.ds(half * part, part)
+        arrive(halves[half])
+        update = upd_part[here, columns(me)]
+        for s in range(1, n):
+            update += upd_recv[s, here]
+        upd_all[ctx, here] = update
+        own = upd_all.at[ctx, here]
+        merged_tokens[here, :] = merged[here, :] + update
+        far = [
+            to("ctx", peer(ctx, s, m), own, own, ug_a, half * m + s // 2) for s in range(2, m, 2)
+        ]
+        firsts.append((far, [to("ctx", mate, own, own, ug_b, half * m)]))
+    for half in range(2):
+        here = pl.ds(half * part, part)
+        far, near = firsts[half]
+        for i, s in enumerate(range(2, m, 2)):
+            far[i].wait_recv()
+            block = upd_all.at[peer(ctx, m - s, m), here]
+            near.append(to("ctx", mate, block, block, ug_b, half * m + i + 1))
     arrive(back_copies)
-    arrive(upd_copies)
+    arrive(firsts[0][1])
+    arrive(firsts[1][1])
     source = split(upd_all[...].reshape(m * rows, local))
 
     def spread(f, carry):
@@ -322,7 +340,7 @@
         pltpu.VMEM((n, rows, local), f32),
         pltpu.VMEM((m, rows, local), f32),
         sems(n), sems(m), sems(m), sems(m), sems(n), sems(m), sems(n), sems(n), sems(n),
-        sems(m), sems(m), sems(n), sems(m), sems(m),
+        sems(m), sems(m), sems(2 * n), sems(2 * m), sems(2 * m),
     ]
     vmem = pl.BlockSpec(memory_space=pltpu.VMEM)
     return pl.pallas_call(

time: 170 us -> 166 us (0.976)
  Pallas kernels: 163 us -> 160 us
    pallas_call x1, Pallas kernels: 163 us -> 160 us  [per_device(): pl.pallas_call(functools.partial(kernel, n, m), out_shape=(jax.ShapeDtype...]
where the time goes in v1:
time: 166 us
  Pallas kernels  160 us (96%)
  local copies, waits for them, and re-layouts  5.64 us (3%)
    pallas_call x1, Pallas kernels, per_device(): pl.pallas_call(functools.partial(kernel, n, m), out_shape=(jax.ShapeDtype...  160 us
    unnamed x2, local copies, waits for them, and re-layouts  3.93 us

profile of v1, /device:TPU:29, one launch (start us, length us, event | category | flops | bytes accessed | tf_op | source)
XLA Modules:
  0.0 165.8 jit_solution(4790960579041661028)
XLA Ops:
  0.6 1.7 %copy.12.index_col = s32[1024,1]{1,0:T(8,128)} copy(s32[1024,1]{0,1:T(1,128)} %bitcast.2) | data formatting | bytes 8192 | tf_op jit(solution)/shard_map/reshape | solution.py:358
  2.3 159.5 %shard_map.113 = (f32[1024,256]{1,0:T(8,128)}, f32[256,256]{1,0:T(8,128)}) custom-call(f32[1024,1024]{1,0:T(8,128)} %frames.1, s32[1,1024]{1,0:T(1,128)} %bitcast.3, s32[1024,1]{1,0:T(8,128)} %copy.12.index_col, f32[1024,256]{1,0:T(8,128)} %fq.1, f32[1024,256]{1,0:T(8,128)} %fk.1, f32[1024,256]{1,0:T(8,128)} %fv.1, f32[256,1024]{1,0:T(8,128)} %fo.1, ...), custom_call_target="tpu_custom_call" | custom-call | tf_op jit(solution)/shard_map/pallas_call | solution.py:346
  161.9 2.3 %copy.15 = f32[1024,256]{1,0:T(8,128)} copy(f32[1024,256]{1,0:T(8,128)} %get-tuple-element.4) | data formatting | bytes 2097152
  164.1 1.7 %copy.16 = f32[256,256]{1,0:T(8,128)} copy(f32[256,256]{1,0:T(8,128)} %get-tuple-element.5) | data formatting | bytes 524288
